TPU v7x, 32 devices: a whole 2x2x4 slice. The times are simulated.
32 devices in a mesh: dp: 8 (over y, x, core), mp: 4 (over z).
Axes of the slice: x: 2, y: 2, z: 4, core: 2. Of those that a mesh axis runs over, the one named last changes fastest.
Arguments:
- tokens: bfloat16 [32, 577, 768], P(('dp', 'mp')), may hold values from -6 to 6
- lengths: int32 [32], P('dp'), may hold values from 257 to 577, as said below
- attention_norm_gain: float32 [768], replicated, may hold values from 0.5 to 1.5
- feedforward_norm_gain: float32 [768], replicated, may hold values from 0.5 to 1.5
- w_query: bfloat16 [768, 768], P(None, 'mp'), may hold values from -0.21875 to 0.21875
- w_key: bfloat16 [768, 768], P(None, 'mp'), may hold values from -0.21875 to 0.21875
- w_value: bfloat16 [768, 768], P(None, 'mp'), may hold values from -0.21875 to 0.21875
- w_out: bfloat16 [768, 768], P('mp'), may hold values from -1.75 to 1.75
- w_gate: bfloat16 [768, 2048], P(None, 'mp'), may hold values from -0.21875 to 0.21875
- w_up: bfloat16 [768, 2048], P(None, 'mp'), may hold values from -0.21875 to 0.21875
- w_down: bfloat16 [2048, 768], P('mp'), may hold values from -0.125 to 0.125
- cotangent: bfloat16 [32, 577, 768], P(('dp', 'mp')), may hold values from -6 to 6
Outputs:
- block_out: float32 [32, 577, 768], P(('dp', 'mp'))
- input_grad: float32 [32, 577, 768], P(('dp', 'mp'))
- grad_gain_attn: float32 [768], replicated
- grad_gain_mlp: float32 [768], replicated
- grad_query: float32 [768, 768], P(None, 'mp')
- grad_key: float32 [768, 768], P(None, 'mp')
- grad_value: float32 [768, 768], P(None, 'mp')
- grad_out: float32 [768, 768], P('mp')
- grad_gate: float32 [768, 2048], P(None, 'mp')
- grad_up: float32 [768, 2048], P(None, 'mp')
- grad_down: float32 [2048, 768], P('mp')
Inputs may be any that keep to these rules, and one draw needn't show every extreme that they name: `lengths`: each item's length is 257 or 577; both occur in every draw.
All inputs are finite; a program needn't handle non-finite values.
Results may differ from a plain program's by a relative error of at most 0.015.
Values may be sent and summed in bfloat16 or wider, within the bound.
A program may use at most 128 MiB of HBM per device.

v0:
```python
import jax
import jax.numpy as jnp
from jax import lax
from jax.sharding import PartitionSpec as P

HEAD = 64


EPS = 1e-05
NEG = -1e30


def tables(length):
    position = jnp.arange(length).astype(jnp.float32)
    index = jnp.arange(HEAD // 2).astype(jnp.float32)
    freq = 10000.0 ** (-2.0 * index / HEAD)
    angle = position[:, None] * freq[None, :]
    angle = jnp.concatenate([angle, angle], axis=-1)
    return (jnp.cos(angle), jnp.sin(angle))


def turn(values):
    half = values.shape[-1] // 2
    return jnp.concatenate([-values[..., half:], values[..., :half]], axis=-1)


def rotate(values, cosine, sine):
    return values * cosine[:, None, :] + turn(values) * sine[:, None, :]


def unrotate(values, cosine, sine):
    return values * cosine[:, None, :] - turn(values * sine[:, None, :])


def inner_rows(left, right):
    return lax.dot_general(
        left, right, (((0,), (0,)), ((), ())), preferred_element_type=jnp.float32
    )


def by_transpose(left, right):
    return lax.dot_general(
        left, right, (((1,), (1,)), ((), ())), preferred_element_type=jnp.float32
    )


def scores_of(query, keys, length):
    seq = query.shape[0]
    scores = jnp.einsum("qhd,khd->hqk", query, keys, preferred_element_type=jnp.float32)
    scores = scores * (1.0 / jnp.sqrt(jnp.float32(HEAD)))
    position = jnp.arange(seq)
    allowed = (position[None, :] <= position[:, None]) & (position[None, :] < length)
    return jnp.where(allowed[None], scores, NEG)


def per_device(
    tokens,
    lengths,
    attention_norm_gain,
    feedforward_norm_gain,
    w_query,
    w_key,
    w_value,
    w_out,
    w_gate,
    w_up,
    w_down,
    cotangent,
):
    own_items, seq, width = tokens.shape
    group = lengths.shape[0]
    heads_here = w_query.shape[1] // HEAD
    head_cols = heads_here * HEAD
    units = w_gate.shape[1]
    own_lengths = lax.dynamic_slice_in_dim(lengths, lax.axis_index("mp") * own_items, own_items)
    cosine, sine = tables(seq)
    full_input_rows = tokens.astype(jnp.float32)
    first_inverse_norm = lax.rsqrt(
        jnp.mean(full_input_rows * full_input_rows, axis=-1, keepdims=True) + EPS
    )
    first_centered_input = full_input_rows * first_inverse_norm
    first_normed_rows = (first_centered_input * attention_norm_gain).astype(jnp.bfloat16)
    rows_one = lax.all_gather(first_normed_rows, "mp", axis=0, tiled=True).reshape(
        group * seq, width
    )
    query = rotate(
        jnp.dot(rows_one, w_query, preferred_element_type=jnp.float32).reshape(
            group, seq, heads_here, HEAD
        ),
        cosine,
        sine,
    ).astype(jnp.bfloat16)
    keys = rotate(
        jnp.dot(rows_one, w_key, preferred_element_type=jnp.float32).reshape(
            group, seq, heads_here, HEAD
        ),
        cosine,
        sine,
    ).astype(jnp.bfloat16)
    values = (
        jnp.dot(rows_one, w_value, preferred_element_type=jnp.float32)
        .astype(jnp.bfloat16)
        .reshape(group, seq, heads_here, HEAD)
    )

    def attend(item):
        query_item, key_item, value_item, length = item
        scores = scores_of(query_item, key_item, length)
        peak = jnp.max(scores, axis=-1, keepdims=True)
        total = peak + jnp.log(jnp.sum(jnp.exp(scores - peak), axis=-1, keepdims=True))
        probs = jnp.exp(scores - total)
        context = jnp.einsum(
            "hqk,khd->qhd",
            probs.astype(jnp.bfloat16),
            value_item,
            preferred_element_type=jnp.float32,
        )
        return (context.astype(jnp.bfloat16), total[..., 0])

    context, log_total = lax.map(attend, (query, keys, values, lengths))
    context_rows = context.reshape(group, seq, head_cols)
    count = own_items * lax.axis_size("mp")
    piece = context_rows
    first_hidden_state = full_input_rows + lax.psum_scatter(
        jnp.dot(
            piece.reshape(count * seq, head_cols), w_out, preferred_element_type=jnp.float32
        ).reshape(count, seq, width),
        "mp",
        scatter_dimension=0,
        tiled=True,
    )
    second_inverse_norm = lax.rsqrt(
        jnp.mean(first_hidden_state * first_hidden_state, axis=-1, keepdims=True) + EPS
    )
    second_centered_input = first_hidden_state * second_inverse_norm
    second_normed_rows = (second_centered_input * feedforward_norm_gain).astype(jnp.bfloat16)
    rows_two = lax.all_gather(second_normed_rows, "mp", axis=0, tiled=True).reshape(
        group * seq, width
    )
    gate = jnp.dot(rows_two, w_gate, preferred_element_type=jnp.float32)
    upper = jnp.dot(rows_two, w_up, preferred_element_type=jnp.float32)
    sigma = jax.nn.sigmoid(gate)
    active = gate * sigma
    hidden = (active * upper).astype(jnp.bfloat16)
    hidden_rows = hidden.reshape(group, seq, units)
    count = lax.axis_size("mp") * own_items
    piece = hidden_rows
    block_out = first_hidden_state + lax.psum_scatter(
        jnp.dot(piece.reshape(count * seq, units), w_down, preferred_element_type=jnp.float32)
        .reshape(count, seq, width)
        .astype(jnp.bfloat16),
        "mp",
        scatter_dimension=0,
        tiled=True,
    ).astype(jnp.float32)
    position = jnp.arange(seq)
    valid = (position[None, :] < own_lengths[:, None]).astype(jnp.float32)
    grad_y = cotangent.astype(jnp.float32) * valid[:, :, None]
    grad_rows = lax.all_gather(grad_y.astype(jnp.bfloat16), "mp", axis=0, tiled=True).reshape(
        group * seq, width
    )
    grad_hidden = by_transpose(grad_rows, w_down)
    grad_down = inner_rows(hidden, grad_rows)
    grad_gate_rows = (grad_hidden * upper * sigma * (1.0 + gate * (1.0 - sigma))).astype(
        jnp.bfloat16
    )
    grad_up_rows = (grad_hidden * active).astype(jnp.bfloat16)
    grad_gate = inner_rows(rows_two, grad_gate_rows)
    grad_up = inner_rows(rows_two, grad_up_rows)
    gate_items = grad_gate_rows.reshape(group, seq, units)
    up_items = grad_up_rows.reshape(group, seq, units)
    count = own_items * lax.axis_size("mp")
    gate_piece = gate_items.reshape(count * seq, units)
    up_piece = up_items.reshape(count * seq, units)
    summed = by_transpose(gate_piece, w_gate) + by_transpose(up_piece, w_up)
    gradient_second_normed = lax.psum_scatter(
        summed.reshape(count, seq, width), "mp", scatter_dimension=0, tiled=True
    )
    feedforward_gain_shard = jnp.sum(gradient_second_normed * second_centered_input, axis=(0, 1))
    second_scaled_rows = gradient_second_normed * feedforward_norm_gain
    grad_one = grad_y + second_inverse_norm * (
        second_scaled_rows
        - second_centered_input
        * jnp.mean(second_scaled_rows * second_centered_input, axis=-1, keepdims=True)
    )
    attn_rows = lax.all_gather(grad_one.astype(jnp.bfloat16), "mp", axis=0, tiled=True).reshape(
        group * seq, width
    )
    grad_context = by_transpose(attn_rows, w_out).astype(jnp.bfloat16)
    grad_out = inner_rows(context.reshape(group * seq, head_cols), attn_rows)
    grad_context = grad_context.reshape(group, seq, heads_here, HEAD)

    def attend_back(item):
        query_item, key_item, value_item, length, total, grad_item = item
        scores = scores_of(query_item, key_item, length)
        probs = jnp.exp(scores - total[..., None])
        grad_probs = jnp.einsum(
            "qhd,khd->hqk", grad_item, value_item, preferred_element_type=jnp.float32
        )
        grad_value_item = jnp.einsum(
            "hqk,qhd->khd",
            probs.astype(jnp.bfloat16),
            grad_item,
            preferred_element_type=jnp.float32,
        )
        grad_scores = (
            probs * (grad_probs - jnp.sum(probs * grad_probs, axis=-1, keepdims=True))
        ).astype(jnp.bfloat16)
        factor = 1.0 / jnp.sqrt(jnp.float32(HEAD))
        grad_query_item = (
            jnp.einsum("hqk,khd->qhd", grad_scores, key_item, preferred_element_type=jnp.float32)
            * factor
        )
        grad_key_item = (
            jnp.einsum("hqk,qhd->khd", grad_scores, query_item, preferred_element_type=jnp.float32)
            * factor
        )
        grad_query_item = unrotate(grad_query_item, cosine, sine).astype(jnp.bfloat16)
        grad_key_item = unrotate(grad_key_item, cosine, sine).astype(jnp.bfloat16)
        return (grad_query_item, grad_key_item, grad_value_item.astype(jnp.bfloat16))

    grad_q, grad_k, grad_v = lax.map(
        attend_back, (query, keys, values, lengths, log_total, grad_context)
    )
    grad_q = grad_q.reshape(group * seq, head_cols)
    grad_k = grad_k.reshape(group * seq, head_cols)
    grad_v = grad_v.reshape(group * seq, head_cols)
    grad_query = inner_rows(rows_one, grad_q)
    grad_key = inner_rows(rows_one, grad_k)
    grad_value = inner_rows(rows_one, grad_v)
    q_items = grad_q.reshape(group, seq, head_cols)
    k_items = grad_k.reshape(group, seq, head_cols)
    v_items = grad_v.reshape(group, seq, head_cols)
    count = lax.axis_size("mp") * own_items
    q_piece = q_items.reshape(count * seq, head_cols)
    k_piece = k_items.reshape(count * seq, head_cols)
    v_piece = v_items.reshape(count * seq, head_cols)
    summed = (
        by_transpose(q_piece, w_query)
        + by_transpose(k_piece, w_key)
        + by_transpose(v_piece, w_value)
    )
    gradient_first_normed = lax.psum_scatter(
        summed.reshape(count, seq, width).astype(jnp.bfloat16),
        "mp",
        scatter_dimension=0,
        tiled=True,
    ).astype(jnp.float32)
    attention_gain_shard = jnp.sum(gradient_first_normed * first_centered_input, axis=(0, 1))
    first_scaled_rows = gradient_first_normed * attention_norm_gain
    input_grad = grad_one + first_inverse_norm * (
        first_scaled_rows
        - first_centered_input
        * jnp.mean(first_scaled_rows * first_centered_input, axis=-1, keepdims=True)
    )
    grad_query, grad_key, grad_value, grad_out, grad_gate, grad_up, grad_down = lax.psum(
        (grad_query, grad_key, grad_value, grad_out, grad_gate, grad_up, grad_down), "dp"
    )
    grad_gain_attn, grad_gain_mlp = lax.psum(
        (attention_gain_shard, feedforward_gain_shard), ("dp", "mp")
    )
    return (
        block_out,
        input_grad,
        grad_gain_attn,
        grad_gain_mlp,
        grad_query,
        grad_key,
        grad_value,
        grad_out,
        grad_gate,
        grad_up,
        grad_down,
    )


def solution(mesh):
    in_specs = (
        P(("dp", "mp"), None, None),
        P("dp"),
        P(),
        P(),
        P(None, "mp"),
        P(None, "mp"),
        P(None, "mp"),
        P("mp", None),
        P(None, "mp"),
        P(None, "mp"),
        P("mp", None),
        P(("dp", "mp"), None, None),
    )
    out_specs = (
        P(("dp", "mp"), None, None),
        P(("dp", "mp"), None, None),
        P(),
        P(),
        P(None, "mp"),
        P(None, "mp"),
        P(None, "mp"),
        P("mp", None),
        P(None, "mp"),
        P(None, "mp"),
        P("mp", None),
    )
    return jax.shard_map(
        per_device, mesh=mesh, in_specs=in_specs, out_specs=out_specs, check_vma=False
    )
```

profile of v0, /device:TPU:0, one launch (start us, length us, event | category | flops | bytes accessed | tf_op | source)
XLA Modules:
  0.0 992.0 jit_solution(10035323367812737138)
XLA Ops:
  12.2 73.1 %all-gather.5.cloned.1.call-done = bf16[4,577,768]{2,1,0:T(8,128)(2,1)} async-done(((bf16[1,577,768]{2,1,0:T(8,128)(2,1)}), bf16[4,577,768]{2,1,0:T(8,128)(2,1)}) %all-gather.5.cloned.1.call-update) | async-done | bytes 3545104 | tf_op jit(solution)/shard_map/all_gather | solution.py:83
  85.3 4.7 reshape.282
  90.0 3.4 convolution_convert_fusion.2
  95.6 3.4 fusion.62
  102.6 26.6 %while.26 = (s32[]{:T(128)}, bf16[4,577,3,64]{1,3,2,0:T(8,128)(2,1)}, f32[4,3,577]{2,1,0:T(4,128)S(1)}, bf16[4,577,3,64]{1,3,2,0:T(8,128)(2,1)}, s32[4]{0:T(128)...) while((s32[]{:T(128)}, bf16[4,577,3,64]{1,3,2,0:T(8,128)(2,1)}, ...), condition=%wide.region_4.5_spmd, body=%wide.region_1.4_spmd.sunk | while | flops 267451616 | bytes 14413002 | solution.py:120
  129.3 5.9 fusion.82
  137.9 121.2 %reduce-scatter.5.cloned.1.call-done = f32[1,577,768]{2,1,0:T(8,128)} async-done(((f32[4,577,768]{2,1,0:T(8,128)}), f32[1,577,768]{2,1,0:T(8,128)}) %reduce-scatter.5.cloned.1.call-update) | async-done | bytes 1772560 | tf_op jit(solution)/shard_map/reduce_scatter | solution.py:124
  262.1 70.4 %all-gather.9.cloned.1.call-done = bf16[4,577,768]{2,1,0:T(8,128)(2,1)} async-done(((bf16[1,577,768]{2,1,0:T(8,128)(2,1)}), bf16[4,577,768]{2,1,0:T(8,128)(2,1)}) %all-gather.9.cloned.1.call-update) | async-done | bytes 3545104 | tf_op jit(solution)/shard_map/all_gather | solution.py:159
  332.5 4.8 reshape.285
  337.3 66.6 %all-gather.7.cloned.1.call-done = bf16[4,577,768]{2,1,0:T(8,128)(2,1)} async-done(((bf16[1,577,768]{2,1,0:T(8,128)(2,1)}), bf16[4,577,768]{2,1,0:T(8,128)(2,1)}) %all-gather.7.cloned.1.call-update) | async-done | bytes 3545104 | tf_op jit(solution)/shard_map/all_gather | solution.py:137
  403.9 4.7 reshape.284
  408.7 4.2 fusion.89
  415.0 4.9 multiply_convert_fusion.1
  422.1 5.1 convolution_add_fusion
  427.3 6.7 reshape.286
  434.4 5.9 convolution_convert_fusion
  440.3 4.9 convert_element_type.121
  445.3 112.5 %reduce-scatter.9.cloned.1.call-done = f32[1,577,768]{2,1,0:T(8,128)} async-done(((f32[4,577,768]{2,1,0:T(8,128)}), f32[1,577,768]{2,1,0:T(8,128)}) %reduce-scatter.9.cloned.1.call-update) | async-done | bytes 1772560 | tf_op jit(solution)/shard_map/reduce_scatter | solution.py:176
  559.8 68.0 %reduce-scatter.7.cloned.1.call-done = bf16[1,577,768]{2,1,0:T(8,128)(2,1)} async-done(((bf16[4,577,768]{2,1,0:T(8,128)(2,1)}), bf16[1,577,768]{2,1,0:T(8,128)(2,1)}) %reduce-scatter.7.cloned.1.call-update) | async-done | bytes 886288 | tf_op jit(solution)/shard_map/reduce_scatter | solution.py:148
  627.8 4.6 fusion.87
  632.5 71.2 %all-gather.11.cloned.1.call-done = bf16[4,577,768]{2,1,0:T(8,128)(2,1)} async-done(((bf16[1,577,768]{2,1,0:T(8,128)(2,1)}), bf16[4,577,768]{2,1,0:T(8,128)(2,1)}) %all-gather.11.cloned.1.call-update) | async-done | bytes 3545104 | tf_op jit(solution)/shard_map/all_gather | solution.py:186
  703.7 4.7 reshape.287
  708.4 4.3 convolution_convert_fusion.1
  712.7 3.5 reshape.288
  721.7 43.0 %while.27 = (s32[]{:T(128)}, bf16[4,577,3,64]{1,3,2,0:T(8,128)(2,1)}, bf16[4,577,3,64]{1,3,2,0:T(8,128)(2,1)}, bf16[4,577,3,64]{1,3,2,0:T(8,128)(2,1)}, bf16[4,5...) while((s32[]{:T(128)}, ...), condition=%wide.region_12.13_spmd, body=%wide.region_10.12_spmd.sunk | while | flops 656273408 | bytes 45620664 | solution.py:222
  783.6 4.7 convert_element_type.131
  793.4 6.3 fusion.99
  799.7 3.4 fusion.98
  814.4 4.7 copy.56
  819.1 35.4 %reduce-scatter.11.cloned.1.call-done = bf16[1,577,768]{2,1,0:T(8,128)(2,1)} async-done(((bf16[4,577,768]{2,1,0:T(8,128)(2,1)}), bf16[1,577,768]{2,1,0:T(8,128)(2,1)}) %reduce-scatter.11.cloned.1.call-update) | async-done | bytes 886288 | tf_op jit(solution)/shard_map/reduce_scatter | solution.py:243
  861.1 41.3 %all-reduce = (f32[768]{0:T(1024)}, f32[768]{0:T(1024)}) all-reduce(f32[768]{0:T(1024)S(1)} %get-tuple-element.210, f32[768]{0:T(1024)S(1)} %get-tuple-element.208), channel_id=1, replica_groups=mesh['dp'=8,'mp'=4] {'dp','mp'}, use_global_device_ids=true, to_apply=%region_16.17 | all-reduce | flops 1536 | bytes 12288 | tf_op jit(solution)/shard_map/psum | solution.py:259
  902.4 72.6 %all-reduce.4.cloned.1.call-done = (f32[768,192]{0,1:T(8,128)}, f32[768,192]{0,1:T(8,128)}, f32[768,192]{0,1:T(8,128)}, f32[192,768]{1,0:T(8,128)}, f32[768,512]...) async-done(((f32[768,192]{0,1:T(8,128)}, f32[768,192]{0,1:T(8,128)}, f32[768,192]{0,1:T(8,128)}, f32[192,768]{1,0:T(8,128)}, f32[768,512]{1,0:T(8,128)}, ...) | async-done | bytes 7077904 | tf_op jit(solution)/shard_map/psum | solution.py:256
  (267 shorter events, 150.0 us)
Async XLA Ops:
  7.2 407.8 %copy-start = (bf16[512,768]{1,0:T(8,128)(2,1)S(1)}, bf16[512,768]{1,0:T(8,128)(2,1)}, u32[]{:S(2)}) copy-start(bf16[512,768]{1,0:T(8,128)(2,1)} %param.26) | copy-start | bytes 2359300
  7.2 78.1 %all-gather.5.cloned.1.call-start = ((), (), s32[]{:S(2)}) async-start(), calls=%async_computation.4 | async-start | bytes 4485120 | tf_op jit(solution)/shard_map/all_gather | solution.py:83
  11.7 247.3 %reduce-scatter.5.cloned.1.call-start = ((), (), s32[]{:S(2)}) async-start(), calls=%async_computation.5 | async-start | bytes 8970240 | tf_op jit(solution)/shard_map/reduce_scatter | solution.py:124
  12.2 88.5 %copy-start.16 = (f32[577,64]{0,1:T(8,128)}, f32[577,64]{0,1:T(8,128)S(1)}, u32[]{:S(2)}) copy-start(f32[577,64]{0,1:T(8,128)S(1)} %get-tuple-element.478) | copy-start | bytes 443140
  12.2 88.5 %copy-start.18 = (f32[577,64]{0,1:T(8,128)}, f32[577,64]{0,1:T(8,128)S(1)}, u32[]{:S(2)}) copy-start(f32[577,64]{0,1:T(8,128)S(1)} %get-tuple-element.479) | copy-start | bytes 443140
  12.2 77.8 %copy-start.45 = (bf16[768,192]{0,1:T(8,128)(2,1)S(1)}, bf16[768,192]{0,1:T(8,128)(2,1)}, u32[]{:S(2)}) copy-start(bf16[768,192]{0,1:T(8,128)(2,1)} %param.22) | copy-start | bytes 884740
  102.6 26.6 %copy-start.39 = (bf16[192,768]{1,0:T(8,128)(2,1)S(1)}, bf16[192,768]{1,0:T(8,128)(2,1)}, u32[]{:S(2)}) copy-start(bf16[192,768]{1,0:T(8,128)(2,1)} %param.23) | copy-start | bytes 884740
  135.2 123.9 %copy-start.4 = (bf16[1,577,768]{2,1,0:T(8,128)(2,1)S(1)}, bf16[1,577,768]{2,1,0:T(8,128)(2,1)}, u32[]{:S(2)}) copy-start(bf16[1,577,768]{2,1,0:T(8,128)(2,1)} %param.16) | copy-start | bytes 2658820
  135.2 197.3 %all-gather.9.cloned.1.call-start = ((), (), s32[]{:S(2)}) async-start(), calls=%async_computation.8 | async-start | bytes 4485120 | tf_op jit(solution)/shard_map/all_gather | solution.py:159
  136.7 124.2 %copy-start.49 = (f32[768]{0:T(1024)S(1)}, f32[768]{0:T(1024)}, u32[]{:S(2)}) copy-start(f32[768]{0:T(1024)} %param.19) | copy-start | bytes 9220
  137.9 266.1 %all-gather.7.cloned.1.call-start = ((), (), s32[]{:S(2)}) async-start(), calls=%async_computation.6 | async-start | bytes 4485120 | tf_op jit(solution)/shard_map/all_gather | solution.py:137
  262.1 295.7 %reduce-scatter.9.cloned.1.call-start = ((), (), s32[]{:S(2)}) async-start(), calls=%async_computation.9 | async-start | bytes 8970240 | tf_op jit(solution)/shard_map/reduce_scatter | solution.py:176
  337.3 71.4 %copy-start.36 = (bf16[768,512]{1,0:T(8,128)(2,1)S(1)}, bf16[768,512]{1,0:T(8,128)(2,1)}, u32[]{:S(2)}) copy-start(bf16[768,512]{1,0:T(8,128)(2,1)} %param.25) | copy-start | bytes 2359300
  434.0 193.8 %reduce-scatter.7.cloned.1.call-start = ((), (), s32[]{:S(2)}) async-start(), calls=%async_computation.7 | async-start | bytes 4485120 | tf_op jit(solution)/shard_map/reduce_scatter | solution.py:148
  445.2 182.6 %copy-start.30 = (bf16[1,577,768]{2,1,0:T(8,128)(2,1)S(1)}, bf16[1,577,768]{2,1,0:T(8,128)(2,1)}, u32[]{:S(2)}) copy-start(bf16[1,577,768]{2,1,0:T(8,128)(2,1)} %param.27) | copy-start | bytes 2658820
  445.2 258.4 %all-gather.11.cloned.1.call-start = ((), (), s32[]{:S(2)}) async-start(), calls=%async_computation.10 | async-start | bytes 4485120 | tf_op jit(solution)/shard_map/all_gather | solution.py:186
  632.4 76.0 %copy-start.40 = (bf16[192,768]{1,0:T(8,128)(2,1)S(1)}, bf16[192,768]{1,0:T(8,128)(2,1)}, u32[]{:S(2)}) copy-start(bf16[192,768]{1,0:T(8,128)(2,1)} %param.23) | copy-start | bytes 884740
  632.4 222.0 %reduce-scatter.11.cloned.1.call-start = ((), (), s32[]{:S(2)}) async-start(), calls=%async_computation.11 | async-start | bytes 4485120 | tf_op jit(solution)/shard_map/reduce_scatter | solution.py:243
  712.7 9.0 copy-start.7
  712.7 9.0 copy-start.9
  712.7 9.0 copy-start.17
  712.7 9.0 copy-start.19
  764.7 9.6 copy-start.24
  770.4 7.5 copy-start.42
  788.4 186.6 %all-reduce.4.cloned.1.call-start = ((), (), s32[]{:S(2)}) async-start(), calls=%async_computation.12 | async-start | bytes 14155776 | tf_op jit(solution)/shard_map/psum | solution.py:256
  793.4 6.3 copy-start.3
  793.4 6.3 copy-start.11
  814.3 40.1 %copy-start.5 = (bf16[1,577,768]{2,1,0:T(8,128)(2,1)S(1)}, bf16[1,577,768]{2,1,0:T(8,128)(2,1)}, u32[]{:S(2)}) copy-start(bf16[1,577,768]{2,1,0:T(8,128)(2,1)} %param.16) | copy-start | bytes 2658820
  814.4 40.1 %copy-start.48 = (f32[577]{0:T(1024)S(1)}, f32[577]{0:T(1024)}, u32[]{:S(2)}) copy-start(f32[577]{0:T(1024)} %copy-done.47) | copy-start | bytes 6928
  814.4 40.1 %copy-start.50 = (f32[768]{0:T(1024)S(1)}, f32[768]{0:T(1024)}, u32[]{:S(2)}) copy-start(f32[768]{0:T(1024)} %param.18) | copy-start | bytes 9220
  814.4 42.0 %copy-start.20 = (f32[1,577,768]{2,1,0:T(8,128)S(1)}, f32[1,577,768]{2,1,0:T(8,128)}, u32[]{:S(2)}) copy-start(f32[1,577,768]{2,1,0:T(8,128)} %get-tuple-element.262) | copy-start | bytes 5317636
  975.0 6.8 copy-start.35
  (32 other events, 92.4 us)
Sparse Core Ops, SparseCore 0:
  11.8 73.4 all-gather.4
  135.3 123.7 reduce-scatter.4
  261.2 71.2 all-gather.8
  334.5 69.3 all-gather.6
  434.1 123.6 reduce-scatter.8
  560.0 67.7 reduce-scatter.6
  632.5 71.0 all-gather.10
  788.5 65.8 reduce-scatter.10
  859.8 115.1 all-reduce.3
where the time goes:
time: 1000 us; the launch traced here: 992 us
  waiting for transfers between devices  691 us (69%)
  matrix products  113 us (11%)
  local copies, waits for them, and re-layouts  90.4 us (9%)
  blocking collectives  41.3 us (4%)
  other arithmetic  40.8 us (4%)
  between operations  14.6 us (1%)
    reduce_scatter x1, waiting for transfers between devices, per_device(): lax.psum_scatter(jnp.dot(piece.reshape(count * seq, head_cols), w_out, pr...  121 us
    reduce_scatter x1, waiting for transfers between devices, per_device(): lax.psum_scatter(summed.reshape(count, seq, width), 'mp', scatter_dimensi...  113 us
    all_gather x1, waiting for transfers between devices, per_device(): lax.all_gather(first_normed_rows, 'mp', axis=0, tiled=True)  73.1 us
    psum x1, waiting for transfers between devices, per_device(): lax.psum((grad_query, grad_key, grad_value, grad_out, grad_gate, grad_up,...  72.6 us
    all_gather x1, waiting for transfers between devices, per_device(): lax.all_gather(grad_one.astype(jnp.bfloat16), 'mp', axis=0, tiled=True)  71.2 us
    all_gather x1, waiting for transfers between devices, per_device(): lax.all_gather(grad_y.astype(jnp.bfloat16), 'mp', axis=0, tiled=True)  70.4 us
    reduce_scatter x1, waiting for transfers between devices, per_device(): lax.psum_scatter(jnp.dot(piece.reshape(count * seq, units), w_down, prefe...  68 us
    all_gather x1, waiting for transfers between devices, per_device(): lax.all_gather(second_normed_rows, 'mp', axis=0, tiled=True)  66.6 us
  transfers between devices with their start and end apart: 9, of which 9 were waited for; matrix products, arithmetic and copies ran while one was open for 6% of the time, Pallas kernels for 0%

commit v1 on v0

v1 whole, which is shorter than its diff:
```python
import functools

import jax
import jax.numpy as jnp
import numpy as np
from jax import lax
from jax.experimental import pallas as pl
from jax.experimental.pallas import tpu as pltpu
from jax.sharding import PartitionSpec as P

HEAD = 64
EPS = 1e-05
NEG = -1e30
MESH = pl.DeviceIdType.MESH
f32, bf16 = jnp.float32, jnp.bfloat16
HEADS = ((0, 0), (0, 1), (1, 0))
RING = 4


def nn(left, right):
    return lax.dot_general(left, right, (((1,), (0,)), ((), ())), preferred_element_type=f32)


def nt(left, right):
    return lax.dot_general(left, right, (((1,), (1,)), ((), ())), preferred_element_type=f32)


def iota(shape, axis):
    return lax.broadcasted_iota(jnp.int32, shape, axis)


def turned(w, low):
    return jnp.where(low, -pltpu.roll(w, 96, 1), pltpu.roll(w, 32, 1))


def order_table(count):
    return [sorted(range(count), key=lambda s: (abs(s - z), s)) for z in range(count)]


def pick(table, row, column):
    found = 0
    for r, values in enumerate(table):
        for c, value in enumerate(values):
            found = found + jnp.where((row == r) & (column == c), value, 0)
    return found


def kernel(
    mp,
    rows,
    len_ref,
    x_ref,
    dy_ref,
    g1_ref,
    g2_ref,
    cos_ref,
    sin_ref,
    own_ref,
    out_ref,
    dx_ref,
    gains_ref,
    fin_ref,
    w,
    n1,
    n1t,
    n2,
    n2t,
    dyb,
    dyt,
    q,
    k,
    v,
    kt,
    vt,
    ctx,
    ctxt,
    lse,
    mask,
    hb,
    dgu,
    dn,
    dk_sum,
    dv_sum,
    dqt,
    dpack,
    gbuf,
    r1,
    r2,
    r3,
    zb,
    r4,
    total,
    gain_in,
    own_sem,
    z_send,
    z_recv,
    g_send,
    g_recv,
    s_send,
    s_recv,
    z4_send,
    z4_recv,
    fin_sem,
    f_send,
    f_recv,
    gain_send,
    gain_recv,
    credit,
):
    T = rows
    seq, width = x_ref.shape[1], x_ref.shape[2]
    half, quarter, eighth = width // 2, width // 4, width // 8
    blocks = [(a, min(a + 256, T)) for a in range(0, T, 256)]
    dp_at, z = lax.axis_index("dp"), lax.axis_index("mp")
    core, bit1, bit2 = dp_at % 2, (dp_at // 2) % 2, (dp_at // 4) % 2
    partner = dp_at + 1 - 2 * core
    flip1, flip2 = dp_at + 2 - 4 * bit1, dp_at + 4 - 8 * bit2
    near = jnp.where(core == 0, flip1, flip2)
    far = jnp.where(core == 0, flip2, flip1)
    near_bit = jnp.where(core == 0, bit1, bit2)
    far_bit = jnp.where(core == 0, bit2, bit1)
    hops = (near, far, partner)
    table = order_table(mp)

    def at(start, size):
        return pl.ds(pl.multiple_of(start, 16), size)

    half_at = core * half
    quarter_at = half_at + far_bit * quarter
    eighth_at = quarter_at + near_bit * eighth
    gather_rows = (at(eighth_at, eighth), at(quarter_at, quarter), at(half_at, half))
    give_rows = (
        at((1 - core) * half, half),
        at(half_at + (1 - far_bit) * quarter, quarter),
        at(quarter_at + (1 - near_bit) * eighth, eighth),
    )
    keep_rows = (at(half_at, half), at(quarter_at, quarter), at(eighth_at, eighth))

    def remote(src, dst, send, recv, dp_to, z_to):
        return pltpu.make_async_remote_copy(
            src_ref=src,
            dst_ref=dst,
            send_sem=send,
            recv_sem=recv,
            device_id={"dp": dp_to, "mp": z_to},
            device_id_type=MESH,
        )


    def along(kind, shard, side):
        part = w.at[kind, shard, gather_rows[0]]
        return remote(part, part, z_send.at[kind, shard, side], z_recv.at[kind, shard], dp_at, z + 1 - 2 * side)

    def across(kind, shard, stage):
        part = w.at[kind, shard, gather_rows[stage]]
        return remote(part, part, g_send.at[kind, shard, stage], g_recv.at[kind, shard, stage], hops[stage], z)

    def send_own(kind):
        for side, there in ((0, z + 1 < mp), (1, z > 0)):
            pl.when(there)(lambda side=side: along(kind, z, side).start())

    def each_side(distance, act):
        for side, shard, there, onward in (
            (0, z - distance, z - distance >= 0, z + 1 < mp),
            (1, z + distance, z + distance < mp, z > 0),
        ):
            pl.when(there)(functools.partial(act, shard, side, onward))

    def arrive(kind, distance, stage):
        def act(shard, side, onward):
            if stage == 0:
                along(kind, shard, side).wait_recv()
                pl.when(onward)(lambda: along(kind, shard, side).start())
            else:
                across(kind, shard, stage - 1).wait_recv()
            if stage < 3:
                across(kind, shard, stage).start()

        each_side(distance, act)

    def unit_of(n):
        later = n - (mp - 1)
        first = n < mp - 1
        return jnp.where(first, 0, 1 + later % 2), jnp.where(first, n + 1, 1 + later // 2)

    units_in = 3 * (mp - 1)

    def tick(n):
        for stage in range(4):
            m = n - stage

            @pl.when((m >= 0) & (m < units_in))
            def _(m=m, stage=stage):
                kind, distance = unit_of(jnp.maximum(m, 0))
                arrive(kind, distance, stage)

    def gather_drain():
        def each(i, carry):
            kind, shard = i // mp, i % mp
            for side, there in ((0, (shard <= z) & (z + 1 < mp)), (1, (shard >= z) & (z > 0))):
                pl.when(there)(lambda side=side: along(kind, shard, side).wait_send())

            @pl.when(shard != z)
            def _():
                for stage in range(3):
                    across(kind, shard, stage).wait_send()

            return carry

        lax.fori_loop(0, 3 * mp, each, 0)


    units_f = 2 * mp
    units = 3 * mp
    landing = (r1, r2, r3)
    hops_back = (partner, far, near)

    def shard_of(u):
        late = u - units_f
        return jnp.where(u < units_f, pick(table, z, u // 2), (z + 1 + late) % mp)

    def kind_of(u):
        return jnp.where(u < units_f, 1 + u % 2, 0)

    def give(u, stage):
        slot = u % RING
        return remote(
            gbuf.at[slot, give_rows[stage]],
            landing[stage].at[slot],
            s_send.at[slot, stage],
            s_recv.at[slot, stage],
            hops_back[stage],
            z,
        )

    def start_give(u, stage):
        pl.when(u >= RING)(lambda: pl.semaphore_wait(credit.at[stage], 1))
        give(u, stage).start()

    def take(u, stage):
        slot = u % RING
        copy = give(u, stage)
        copy.wait_recv()
        copy.wait_send()
        sums = gbuf[slot, keep_rows[stage], :].astype(f32) + landing[stage][slot].astype(f32)
        sums = sums.astype(bf16)

        @pl.when(u + RING < units)
        def _():
            pl.semaphore_signal(
                credit.at[stage], inc=1, device_id={"dp": hops_back[stage], "mp": z}, device_id_type=MESH
            )

        if stage < 2:
            gbuf[slot, keep_rows[stage], :] = sums
            start_give(u, stage + 1)
            return
        shard, kind = shard_of(u), kind_of(u)

        @pl.when(shard == z)
        def _():
            r4[kind, z] = sums

        @pl.when(shard != z)
        def _():
            zb[u] = sums
            home(u).start()

    def home(u):
        kind = kind_of(u)
        return remote(zb.at[u], r4.at[kind, z], z4_send.at[u], z4_recv.at[kind, z], dp_at, shard_of(u))

    def home_drain():
        def each(u, carry):
            pl.when(shard_of(u) != z)(lambda: home(u).wait_send())
            return carry

        lax.fori_loop(0, units, each, 0)


    def fin_own(kind):
        return pltpu.make_async_copy(total.at[kind], fin_ref.at[kind, gather_rows[0]], fin_sem.at[kind])

    def fin_across(kind, stage):
        src = total.at[kind] if stage == 0 else fin_ref.at[kind, gather_rows[stage]]
        return remote(
            src,
            fin_ref.at[kind, gather_rows[stage]],
            f_send.at[kind, stage],
            f_recv.at[kind, stage],
            hops[stage],
            z,
        )

    def finish(kind, stage):
        if stage == 0:
            for src in range(mp):

                @pl.when(z != src)
                def _(src=src):
                    remote(
                        zb.at[0], r4.at[kind, src], z4_send.at[0], z4_recv.at[kind, src], dp_at, src
                    ).wait_recv()

            sums = r4[kind, 0].astype(f32)
            for src in range(1, mp):
                sums = sums + r4[kind, src].astype(f32)
            total[kind] = sums.astype(bf16)
            fin_own(kind).start()
        else:
            if stage == 1:
                fin_own(kind).wait()
            fin_across(kind, stage - 1).wait_recv()
        if stage < 3:
            fin_across(kind, stage).start()

    def finish_drain(kind):
        for stage in range(3):
            fin_across(kind, stage).wait_send()


    gain_hops = ((partner, z), (far, z), (near, z))

    def gain_copy(stage):
        to = gain_hops[stage]
        return remote(
            gain_in.at[0], gain_in.at[1 + stage], gain_send.at[stage], gain_recv.at[stage], *to
        )

    def gain_along(i, to):
        return remote(
            gain_in.at[0], gain_in.at[3 + i], gain_send.at[2 + i], gain_recv.at[2 + i], dp_at, to
        )

    def gain_step(stage):
        if stage > 0:
            copy = gain_copy(stage - 1)
            copy.wait()
            gain_in[0] = gain_in[0] + gain_in[stage]
        if stage < 3:
            gain_copy(stage).start()
        else:
            for i in range(1, mp):
                gain_along(i, (z + i) % mp).start()

    def gain_end():
        for i in range(1, mp):
            gain_along(i, (z + i) % mp).wait()
        sums = gain_in[0]
        for i in range(1, mp):
            sums = sums + gain_in[3 + i]
        gains_ref[...] = sums


    barrier = pltpu.get_barrier_semaphore()
    for to in (partner, near, far):
        pl.semaphore_signal(barrier, inc=1, device_id={"dp": to, "mp": z}, device_id_type=MESH)
    for i in range(1, mp):
        pl.semaphore_signal(
            barrier, inc=1, device_id={"dp": dp_at, "mp": (z + i) % mp}, device_id_type=MESH
        )
    own = [pltpu.make_async_copy(own_ref.at[kind], w.at[kind, z], own_sem.at[kind]) for kind in range(3)]
    for copy in own:
        copy.start()

    lane = iota((T, 128), 1)
    lower = lane < 64
    low = (lane % 64) < 32
    length = len_ref[z]
    full = seq // 16 * 16

    def padded(ref):
        tail = jnp.broadcast_to(ref[0, full:seq, :].astype(f32), (T - full, width))
        tail = jnp.where(iota((T - full, width), 0) < seq - full, tail, 0.0).astype(bf16)
        return jnp.concatenate([ref[0, 0:full, :], tail], axis=0)

    def scale_of(rows_in):
        return lax.rsqrt(jnp.mean(rows_in * rows_in, axis=-1, keepdims=True) + EPS)

    for copy in own:
        copy.wait()
    pl.semaphore_wait(barrier, 3 + mp - 1)
    send_own(0)

    x = padded(x_ref).astype(f32)
    normed = (x * scale_of(x) * g1_ref[...]).astype(bf16)
    n1[...] = normed
    n1t[...] = normed.T
    out_ref[...] = x
    live = jnp.where(iota((T, width), 0) < length, padded(dy_ref).astype(f32), 0.0).astype(bf16)
    dyb[...] = live
    dyt[...] = live.T
    key_at, query_at = iota((T, T), 0), iota((T, T), 1)
    mask[...] = jnp.where((key_at <= query_at) & (key_at < length), 0.0, NEG)
    ctxt[...] = jnp.zeros_like(ctxt)
    dqt[...] = jnp.zeros_like(dqt)


    def attention(step, carry):
        def point(i):
            tick(jnp.where(step == 0, i, 3 + step if i == 0 else -1))

        cos, sin = cos_ref[...], sin_ref[...]
        s = pick(table, z, step)
        wa = w.at[0, s]
        qkv = nn(n1[...], wa[:, 0:640])
        point(0)

        @pl.when(step == 0)
        def _():
            send_own(1)

        first = qkv[:, 0:128]
        mixed = qkv[:, 128:256]
        keys = qkv[:, 256:384]
        first = (first * cos + turned(first, low) * sin) * 0.125
        mixed = mixed * cos + turned(mixed, low) * sin
        keys = keys * cos + turned(keys, low) * sin
        q[s, 0] = first.astype(bf16)
        q[s, 1] = jnp.where(lower, mixed * 0.125, 0.0).astype(bf16)
        k[s, 0] = keys.astype(bf16)
        k[s, 1] = jnp.where(lower, pltpu.roll(mixed, 64, 1), 0.0).astype(bf16)
        v[s, 0] = qkv[:, 384:512].astype(bf16)
        v[s, 1] = jnp.where(lower, qkv[:, 512:640], 0.0).astype(bf16)
        for tile in range(2):
            kt[s, tile] = k[s, tile].T
            vt[tile] = v[s, tile].T
        for h, (tile, side) in enumerate(HEADS):
            qh = q[s, tile]
            if tile == 0:
                qh = jnp.where(lower if side == 0 else ~lower, qh, jnp.zeros_like(qh))
            for a, b in blocks:
                scores = nt(k[s, tile, 0:b, :], qh[a:b]) + mask[0:b, a:b]
                peak = jnp.max(scores, axis=0, keepdims=True)
                e = jnp.exp(scores - peak)
                norm = jnp.sum(e, axis=0, keepdims=True)
                c = nn(vt[tile, 64 * side : 64 * side + 64, 0:b], e.astype(bf16))
                ctxt[64 * h : 64 * h + 64, a:b] = c * (1.0 / norm)
                lse[s, h : h + 1, a:b] = peak + jnp.log(norm)
            point(1 + h)
        last = ctxt[128:256, :].T
        ctx[s, :, 0:128] = jnp.where(lower, 0.0, pltpu.roll(last, 64, 1)).astype(bf16)
        ctx[s, :, 128:256] = ctxt[0:128, :].T.astype(bf16)
        out_ref[...] += nt(ctx[s], wa[:, 512:768])

        @pl.when(step == 0)
        def _():
            send_own(2)

        return carry

    lax.fori_loop(0, mp, attention, 0)

    x1 = out_ref[...]
    dx_ref[...] = x1
    normed = (x1 * scale_of(x1) * g2_ref[...]).astype(bf16)
    n2[...] = normed
    n2t[...] = normed.T
    dn[...] = jnp.zeros_like(dn)


    def feed(step, carry):
        s = pick(table, z, step)
        w0, w1 = w.at[1, s], w.at[2, s]
        u0, u1 = 2 * step, 2 * step + 1
        gu = nn(n2[...], w0[...])
        rest = nn(n2[...], w1[:, 0:256])
        dh = nn(dyb[...], w1[:, 256:768])
        for i in range(2):
            cols = slice(256 * i, 256 * i + 256)
            gate = gu[:, cols]
            up = gu[:, 512:768] if i == 0 else rest
            dhid = dh[:, cols]
            sigma = 1.0 / (1.0 + jnp.exp(-gate))
            active = gate * sigma
            hb[:, cols] = (active * up).astype(bf16)
            dgu[:, cols] = (dhid * up * sigma * (1.0 + gate * (1.0 - sigma))).astype(bf16)
            dgu[:, 512 + 256 * i : 768 + 256 * i] = (dhid * active).astype(bf16)
        tick(7 + 2 * step)
        gbuf[u0 % RING] = nn(n2t[...], dgu[:, 0:768]).astype(bf16)
        start_give(u0, 0)

        @pl.when(step >= 1)
        def _():
            take(u0 - 1, 0)
            take(u0 - 2, 1)

        pl.when(step >= 2)(lambda: take(u0 - 3, 2))
        out_ref[...] += nt(hb[...], w1[:, 256:768])
        tick(jnp.where(step < 2, 8 + 2 * step, -1))
        gbuf[u1 % RING, :, 0:256] = nn(n2t[...], dgu[:, 768:1024]).astype(bf16)
        gbuf[u1 % RING, :, 256:768] = nn(dyt[...], hb[...]).astype(bf16)
        start_give(u1, 0)
        take(u0, 0)

        @pl.when(step >= 1)
        def _():
            take(u0 - 1, 1)
            take(u0 - 2, 2)

        dn[...] += nt(dgu[:, 0:768], w0[...]) + nt(dgu[:, 768:1024], w1[:, 0:256])
        return carry

    lax.fori_loop(0, mp, feed, 0)

    x1 = dx_ref[...]
    scale = scale_of(x1)
    hat = x1 * scale
    d2 = dn[...]
    gain_in[0] = jnp.zeros_like(gain_in[0])
    gain_in[0, 1:2, :] = jnp.sum(d2 * hat, axis=0, keepdims=True)
    e = d2 * g2_ref[...]
    dx1 = dyb[...].astype(f32) + scale * (e - hat * jnp.mean(e * hat, axis=-1, keepdims=True))
    dx_ref[...] = dx1
    lowered = dx1.astype(bf16)
    n2[...] = lowered
    n2t[...] = lowered.T
    dn[...] = jnp.zeros_like(dn)


    def back(step, carry):
        u = units_f + step
        slot = u % RING
        cos, sin = cos_ref[...], sin_ref[...]
        s = shard_of(u)
        wa = w.at[0, s]
        dc = nn(n2[...], wa[:, 512:768])
        dc2 = jnp.where(lower, pltpu.roll(dc[:, 0:128], 64, 1), 0.0).astype(bf16)
        dc01 = dc[:, 128:256].astype(bf16)
        for tile in range(2):
            dk_sum[tile] = jnp.zeros((T, 128), f32)
            dv_sum[tile] = jnp.zeros((T, 128), f32)
        for h, (tile, side) in enumerate(HEADS):
            qh = q[s, tile]
            dch = dc01 if tile == 0 else dc2
            if tile == 0:
                here = lower if side == 0 else ~lower
                qh = jnp.where(here, qh, jnp.zeros_like(qh))
                dch = jnp.where(here, dch, jnp.zeros_like(dch))
            for a, b in blocks:
                scores = nt(k[s, tile, 0:b, :], qh[a:b]) + mask[0:b, a:b]
                p = jnp.exp(scores - lse[s, h : h + 1, a:b])
                dprob = nt(v[s, tile, 0:b, :], dch[a:b])
                delta = jnp.sum(p * dprob, axis=0, keepdims=True)
                ds = (p * (dprob - delta)).astype(bf16)
                dv_sum[tile, 0:b, :] += nn(p.astype(bf16), dch[a:b])
                dk_sum[tile, 0:b, :] += nn(ds, qh[a:b])
                dqt[64 * h : 64 * h + 64, a:b] = nn(kt[s, tile, 64 * side : 64 * side + 64, 0:b], ds)
            take(u - 1, h)
            if h < 2:

                @pl.when(step == 0)
                def _(h=h):
                    take(u - 2, h + 1)
                    if h == 0:
                        take(u - 3, 2)

        dq01 = dqt[0:128, :].T * 0.125
        dq2 = dqt[128:256, :].T * 0.125
        dq01 = dq01 * cos - turned(dq01, low) * sin
        dq2 = dq2 * cos - turned(dq2, low) * sin
        dk01 = dk_sum[0] * cos - turned(dk_sum[0], low) * sin
        dk2 = dk_sum[1] * cos - turned(dk_sum[1], low) * sin
        dpack[:, 0:128] = dq01.astype(bf16)
        dpack[:, 128:256] = jnp.where(lower, dq2, pltpu.roll(dk2, 64, 1)).astype(bf16)
        dpack[:, 256:384] = dk01.astype(bf16)
        dpack[:, 384:512] = dv_sum[0].astype(bf16)
        dpack[:, 512:640] = jnp.where(lower, dv_sum[1], 0.0).astype(bf16)
        gbuf[slot, :, 0:512] = nn(n1t[...], dpack[:, 0:512]).astype(bf16)
        gbuf[slot, :, 512:640] = (
            nn(n1t[...], dpack[:, 512:640]) + nn(n2t[...], ctx[s, :, 0:128])
        ).astype(bf16)
        gbuf[slot, :, 640:768] = nn(n2t[...], ctx[s, :, 128:256]).astype(bf16)
        start_give(u, 0)
        for stage in range(3):

            @pl.when(step == 1 + stage)
            def _(stage=stage):
                finish(1, stage)
                finish(2, stage)

        dn[...] += nt(dpack[...], wa[:, 0:640])
        return carry

    lax.fori_loop(0, mp, back, 0)

    take(units - 1, 0)
    x = padded(x_ref).astype(f32)
    scale = scale_of(x)
    hat = x * scale
    d1 = dn[...]
    gain_in[0, 0:1, :] = jnp.sum(d1 * hat, axis=0, keepdims=True)
    gain_step(0)
    e = d1 * g1_ref[...]
    dx_ref[...] += scale * (e - hat * jnp.mean(e * hat, axis=-1, keepdims=True))
    take(units - 1, 1)
    gain_step(1)
    take(units - 1, 2)
    finish(0, 0)
    gain_step(2)
    finish(0, 1)
    gain_step(3)
    finish(0, 2)
    gain_end()
    finish(1, 3)
    finish(2, 3)
    gather_drain()
    home_drain()
    finish(0, 3)
    for kind in range(3):
        finish_drain(kind)


def rotary(rows):
    position = np.arange(rows).astype(np.float32)
    index = np.arange(HEAD // 2).astype(np.float32)
    freq = (np.float32(10000.0) ** (np.float32(-2.0) * index / np.float32(HEAD))).astype(np.float32)
    angle = position[:, None] * freq[None, :]
    angle = np.concatenate([angle] * 4, axis=-1)
    return np.cos(angle).astype(np.float32), np.sin(angle).astype(np.float32)


def layer(mp, lengths, tokens, cotangent, gain1, gain2, own):
    _, seq, width = tokens.shape
    T = (seq + 15) // 16 * 16
    cosine, sine = rotary(T)
    vmem, anywhere = pl.BlockSpec(memory_space=pltpu.VMEM), pl.BlockSpec(memory_space=pl.ANY)
    V, DMA = pltpu.VMEM, pltpu.SemaphoreType.DMA
    half, quarter, eighth = width // 2, width // 4, width // 8
    scratch = [
        V((3, mp, width, width), bf16),
        V((T, width), bf16),
        V((width, T), bf16),
        V((T, width), bf16),
        V((width, T), bf16),
        V((T, width), bf16),
        V((width, T), bf16),
        V((mp, 2, T, 128), bf16),
        V((mp, 2, T, 128), bf16),
        V((mp, 2, T, 128), bf16),
        V((mp, 2, 128, T), bf16),
        V((2, 128, T), bf16),
        V((mp, T, 256), bf16),
        V((256, T), f32),
        V((mp, 8, T), f32),
        V((T, T), f32),
        V((T, 512), bf16),
        V((T, 1024), bf16),
        V((T, width), f32),
        V((2, T, 128), f32),
        V((2, T, 128), f32),
        V((256, T), f32),
        V((T, 640), bf16),
        V((RING, width, width), bf16),
        V((RING, half, width), bf16),
        V((RING, quarter, width), bf16),
        V((RING, eighth, width), bf16),
        V((3 * mp, eighth, width), bf16),
        V((3, mp, eighth, width), bf16),
        V((3, eighth, width), bf16),
        V((3 + mp, 8, width), f32),
        DMA((3,)),
        DMA((3, mp, 2)),
        DMA((3, mp)),
        DMA((3, mp, 3)),
        DMA((3, mp, 3)),
        DMA((RING, 3)),
        DMA((RING, 3)),
        DMA((3 * mp,)),
        DMA((3, mp)),
        DMA((3,)),
        DMA((3, 3)),
        DMA((3, 3)),
        DMA((2 + mp,)),
        DMA((2 + mp,)),
        pltpu.SemaphoreType.REGULAR((3,)),
    ]
    return pl.pallas_call(
        functools.partial(kernel, mp, T),
        out_shape=(
            jax.ShapeDtypeStruct((T, width), f32),
            jax.ShapeDtypeStruct((T, width), f32),
            jax.ShapeDtypeStruct((8, width), f32),
            jax.ShapeDtypeStruct((3, width, width), bf16),
        ),
        in_specs=[pl.BlockSpec(memory_space=pltpu.SMEM)] + [vmem] * 6 + [anywhere],
        out_specs=[vmem, vmem, vmem, anywhere],
        scratch_shapes=scratch,
        compiler_params=pltpu.CompilerParams(
            collective_id=0, has_side_effects=True, vmem_limit_bytes=63 * 2**20
        ),
    )(lengths, tokens, cotangent, gain1[None], gain2[None], jnp.asarray(cosine), jnp.asarray(sine), own)


def per_device(mp, dp, tokens, lengths, gain1, gain2, wq, wk, wv, wo, wg, wu, wd, cotangent):
    seq = tokens.shape[1]
    wot, wdt = wo.T, wd.T
    own = jnp.stack(
        [
            jnp.concatenate(
                [wq, wk[:, 128:], wk[:, :128], wv, wot[:, 128:], wot[:, :128]], axis=1
            ),
            jnp.concatenate([wg, wu[:, :256]], axis=1),
            jnp.concatenate([wu[:, 256:], wdt], axis=1),
        ]
    )
    out, dx, gains, fin = layer(mp, lengths, tokens, cotangent, gain1, gain2, own)
    fin, gains = fin.astype(f32), gains[0:2]
    if dp > 8:
        groups = [[8 * i + j for i in range(dp // 8)] for j in range(8)]
        fin, gains = lax.psum((fin, gains), "dp", axis_index_groups=groups)
    a, f0, f1 = fin[0], fin[1], fin[2]
    return (
        out[None, :seq],
        dx[None, :seq],
        gains[0],
        gains[1],
        a[:, 0:192],
        jnp.concatenate([a[:, 256:384], a[:, 192:256]], axis=1),
        a[:, 384:576],
        jnp.concatenate([a[:, 640:768], a[:, 576:640]], axis=1).T,
        f0[:, 0:512],
        jnp.concatenate([f0[:, 512:], f1[:, :256]], axis=1),
        f1[:, 256:].T,
    )


def solution(mesh):
    rows, cols, items = P("mp", None), P(None, "mp"), P(("dp", "mp"), None, None)
    return jax.shard_map(
        functools.partial(per_device, mesh.shape["mp"], mesh.shape["dp"]),
        mesh=mesh,
        in_specs=(items, P("dp"), P(), P(), cols, cols, cols, rows, cols, cols, rows, items),
        out_specs=(items, items, P(), P(), cols, cols, cols, rows, cols, cols, rows),
        check_vma=False,
    )
```

time: 1000 us -> 252 us (0.25)
  waiting for transfers between devices: 691 us -> 0 us
  Pallas kernels: 0 us -> 208 us
  matrix products: 113 us -> 0 us
  local copies, waits for them, and re-layouts: 90.4 us -> 36.4 us
  blocking collectives: 41.3 us -> 0 us
  other arithmetic: 40.8 us -> 5.35 us
  between operations: 14.6 us -> 0.82 us
    reduce_scatter x4 -> x0, waiting for transfers between devices: 337 us -> none  [the longest x1 121 us: per_device(): lax.psum_scatter(jnp.dot(piece.reshape(count * seq, head_cols), w_out, pr...]
    all_gather x4 -> x0, waiting for transfers between devices: 281 us -> none  [the longest x1 73.1 us: per_device(): lax.all_gather(first_normed_rows, 'mp', axis=0, tiled=True)]
    pallas_call x0 -> x1, Pallas kernels: none -> 208 us  [layer(): pl.pallas_call(functools.partial(kernel, mp, T), out_shape=(jax.ShapeDtyp...]
    dot_general x49 -> x0, matrix products: 113 us -> none  [the longest x7 22.1 us: by_transpose(): lax.dot_general(left, right, (((1,), (1,)), ((), ())), preferred_element_...]
    psum x1 -> x0, waiting for transfers between devices: 72.6 us -> none  [per_device(): lax.psum((grad_query, grad_key, grad_value, grad_out, grad_gate, grad_up,...]
    psum x1 -> x0, blocking collectives: 41.3 us -> none  [per_device(): lax.psum((attention_gain_shard, feedforward_gain_shard), ('dp', 'mp'))]
    reshape x7 -> x0, local copies, waits for them, and re-layouts: 30.2 us -> none  [the longest x1 6.66 us: per_device(): summed.reshape(count, seq, width)]
    convert_element_type x11 -> x1, other arithmetic: 15.9 us -> 0.6 us  [per_device(): fin, gains = (fin.astype(f32), gains[0:2])]
  transfers between devices with their start and end apart: 9 -> 0, of which waited for: 9 -> 0; matrix products, arithmetic and copies ran while one was open for 6% -> 0% of each run, Pallas kernels for 0% -> 0%
where the time goes in v1:
time: 252 us; the launch traced here: 251 us
  Pallas kernels  208 us (83%)
  local copies, waits for them, and re-layouts  36.4 us (14%)
  other arithmetic  5.35 us (2%)
    pallas_call x1, Pallas kernels, layer(): pl.pallas_call(functools.partial(kernel, mp, T), out_shape=(jax.ShapeDtyp...  208 us
    unnamed x27, local copies, waits for them, and re-layouts  17.1 us

profile of v1, /device:TPU:0, one launch (start us, length us, event | category | flops | bytes accessed | tf_op | source)
XLA Modules:
  0.0 250.9 jit_solution(1109481112875094836)
XLA Ops:
  0.7 1.3 broadcast_in_dim.12.g1_ref
  2.0 1.3 broadcast_in_dim.13.g2_ref
  3.3 0.9 slice.72
  4.3 0.9 slice.73
  5.4 1.1 copy.28
  6.6 0.2 copy.29
  6.8 0.2 copy.27
  7.0 0.5 concatenate.18
  7.6 0.5 copy-done.4
  8.1 0.3 copy.30
  8.4 1.2 fusion.3
  9.7 2.0 pad_maximum_fusion.own_ref
  11.7 208.3 %shard_map.221 = (f32[592,768]{1,0:T(8,128)}, f32[592,768]{1,0:T(8,128)}, f32[8,768]{1,0:T(8,128)}, bf16[3,768,768]{2,1,0:T(8,128)(2,1)}) custom-call(s32[4]{0:T(128)} %len_ref.1, bf16[1,577,768]{2,1,0:T(8,128)(2,1)} %x_ref.1, bf16[1,577,768]{2,1,0:T(8,128)(2,1)} %dy_ref.1, f32[1,768]{1,0:T(1,128)} %broadcast_in_dim.12.g1_ref, ...), custom_call_target="tpu_custom_call" | custom-call | tf_op jit(solution)/shard_map/pallas_call | solution.py:678
  220.0 1.6 slice_bitcast_fusion.4
  221.6 3.0 %copy.31 = f32[1,577,768]{2,0,1:T(1,128)} copy(f32[1,577,768]{2,1,0:T(8,128)S(1)} %slice_bitcast_fusion.4) | data formatting | bytes 3545088
  224.6 1.4 slice_reduce_fusion
  226.2 3.0 %copy.32 = f32[1,577,768]{2,0,1:T(1,128)} copy(f32[1,577,768]{2,1,0:T(8,128)S(1)} %slice_bitcast_fusion.3) | data formatting | bytes 3545088
  229.2 0.6 convert_element_type.3
  229.8 1.9 slice_bitcast_fusion
  231.7 1.3 slice_bitcast_fusion.5
  233.1 3.0 %copy.37 = f32[512,768]{1,0:T(8,128)} copy(f32[512,768]{0,1:T(8,128)} %slice_bitcast_fusion.5) | data formatting | bytes 3145728
  236.1 1.2 slice.106
  237.3 2.7 %slice.105 = f32[768,512]{1,0:T(8,128)} slice(f32[768,768]{1,0:T(8,128)} %get-tuple-element.33), slice={[0:768], [0:512]} | slice | bytes 3145728 | tf_op jit(solution)/shard_map/slice | solution.py:722
  240.0 1.4 pad_maximum_fusion.1
  241.3 1.0 fusion.1
  242.3 0.9 fusion
  243.2 1.0 fusion.2
  244.2 2.2 copy.35
  246.4 1.2 maximum_bitcast_fusion.2
  247.7 1.1 copy.36
  248.8 1.1 copy.34
  249.8 1.1 copy.33
  (21 shorter events, 0.8 us)
Async XLA Ops:
  0.6 6.1 %copy-start.6 = (bf16[192,768]{1,0:T(8,128)(2,1)S(1)}, bf16[192,768]{1,0:T(8,128)(2,1)}, u32[]{:S(2)}) copy-start(bf16[192,768]{1,0:T(8,128)(2,1)} %param.21) | copy-start | bytes 884740
  0.7 5.9 %copy-start.5 = (bf16[768,192]{0,1:T(8,128)(2,1)S(1)}, bf16[768,192]{0,1:T(8,128)(2,1)}, u32[]{:S(2)}) copy-start(bf16[768,192]{0,1:T(8,128)(2,1)} %param.20) | copy-start | bytes 884740
  6.9 1.1 copy-start.4
  7.6 2.0 copy-start.3
  221.6 4.5 %copy-start.1 = (f32[592,768]{1,0:T(8,128)S(1)}, f32[592,768]{1,0:T(8,128)}, u32[]{:S(2)}) copy-start(f32[592,768]{1,0:T(8,128)} %get-tuple-element.16) | copy-start | bytes 5455876
  226.2 3.0 %copy-start = (bf16[3,768,768]{2,1,0:T(8,128)(2,1)S(1)}, bf16[3,768,768]{2,1,0:T(8,128)(2,1)}, u32[]{:S(2)}) copy-start(bf16[3,768,768]{2,1,0:T(8,128)(2,1)} %get-tuple-element.18) | copy-start | bytes 10616836
  246.4 2.3 copy-start.2

commit v2 on v1

v2 whole, which is shorter than its diff:
```python
import functools

import jax
import jax.numpy as jnp
import numpy as np
from jax import lax
from jax.experimental import pallas as pl
from jax.experimental.pallas import tpu as pltpu
from jax.sharding import PartitionSpec as P

HEAD = 64
EPS = 1e-05
NEG = -1e30
MESH = pl.DeviceIdType.MESH
f32, bf16 = jnp.float32, jnp.bfloat16
HEADS = ((0, 1), (1, 0), (1, 1))
SLOTS = (3, 6, 8, 12)
STEPS = (3, 3, 2)

PLAN = {
    ("P", 0, 0): (("s", 0),),
    ("A", 0, 4): (("s", 1),),
    ("A", 1, 0): (("z", 0, 1), ("g", 0, 1, 0), ("z", 1, 1), ("g", 1, 1, 0), ("g", 0, 1, 1), ("z", 0, 2), ("g", 0, 2, 0), ("g", 1, 1, 1), ("z", 1, 2), ("g", 1, 2, 0), ("g", 0, 1, 2), ("g", 0, 2, 1), ("z", 0, 3), ("g", 0, 3, 0), ("g", 0, 1, 3), ("s", 2),),
    ("A", 1, 3): (("g", 1, 1, 2), ("z", 1, 3), ("g", 1, 3, 0),),
    ("A", 1, 4): (("g", 1, 2, 1),),
    ("A", 2, 0): (("g", 1, 1, 3), ("g", 0, 2, 2), ("g", 0, 3, 1), ("z", 2, 1), ("g", 0, 2, 3), ("g", 2, 1, 0),),
    ("A", 2, 1): (("g", 1, 3, 1),),
    ("A", 3, 0): (("g", 1, 2, 2), ("g", 0, 3, 2), ("g", 1, 2, 3), ("z", 2, 2), ("g", 2, 2, 0), ("g", 0, 3, 3),),
    ("A", 3, 1): (("g", 2, 1, 1),),
    ("A", 3, 4): (("g", 2, 1, 2),),
    ("F", 0, 0): (("g", 1, 3, 2),),
    ("F", 0, 1): (("g", 2, 2, 1), ("g", 1, 3, 3),),
    ("F", 0, 2): (("z", 2, 3), ("g", 2, 3, 0),),
    ("F", 0, 3): (("g", 2, 2, 2),),
    ("F", 0, 4): (("t", 0, 0),),
    ("F", 1, 1): (("t", 1, 0),),
    ("F", 1, 2): (("g", 2, 3, 1),),
    ("F", 1, 4): (("t", 2, 0),),
    ("F", 2, 0): (("g", 2, 3, 2), ("t", 0, 1),),
    ("F", 2, 1): (("t", 3, 0),),
    ("F", 2, 2): (("t", 1, 1),),
    ("F", 2, 4): (("t", 4, 0), ("t", 2, 1),),
    ("F", 3, 1): (("t", 0, 2), ("t", 5, 0),),
    ("F", 3, 3): (("t", 3, 1),),
    ("F", 3, 4): (("t", 1, 2), ("t", 6, 0),),
    ("B", 0, 0): (("t", 7, 0), ("t", 4, 1),),
    ("B", 0, 1): (("t", 2, 2),),
    ("B", 0, 3): (("t", 5, 1),),
    ("B", 0, 5): (("t", 3, 2),),
    ("B", 0, 7): (("t", 6, 1),),
    ("B", 1, 1): (("t", 8, 0), ("t", 7, 1),),
    ("B", 1, 2): (("t", 4, 2),),
    ("B", 1, 3): (("t", 5, 2),),
    ("B", 1, 4): (("t", 6, 2),),
    ("B", 1, 7): (("t", 8, 1),),
    ("B", 1, 8): (("t", 7, 2),),
    ("B", 2, 1): (("t", 9, 0),),
    ("B", 2, 2): (("t", 8, 2),),
    ("B", 2, 6): (("t", 9, 1),),
    ("B", 3, 1): (("t", 10, 0),),
    ("B", 3, 2): (("t", 9, 2),),
    ("B", 3, 3): (("f", 1, 0),),
    ("B", 3, 6): (("t", 10, 1),),
    ("B", 3, 8): (("f", 1, 1), ("f", 2, 0),),
    ("E", 0, 1): (("n", 0),),
    ("E", 0, 2): (("t", 11, 0), ("t", 10, 2), ("n", 1),),
    ("E", 0, 6): (("f", 1, 2),),
    ("E", 0, 7): (("f", 2, 1), ("f", 1, 3), ("t", 11, 1), ("n", 2), ("f", 2, 2), ("t", 11, 2), ("f", 0, 0), ("n", 3), ("f", 2, 3), ("n", 4), ("f", 0, 1), ("f", 0, 2), ("f", 0, 3),),
}


def nn(left, right):
    return lax.dot_general(left, right, (((1,), (0,)), ((), ())), preferred_element_type=f32)


def nt(left, right):
    return lax.dot_general(left, right, (((1,), (1,)), ((), ())), preferred_element_type=f32)


def iota(shape, axis):
    return lax.broadcasted_iota(jnp.int32, shape, axis)


def turned(w, low):
    return jnp.where(low, -pltpu.roll(w, 96, 1), pltpu.roll(w, 32, 1))


def swap(w):
    return pltpu.roll(w, 64, 1)


def order_table(count):
    def key(z):
        return lambda s: (abs(s - z), s if z < count / 2 else -s)

    return [sorted(range(count), key=key(z)) for z in range(count)]


def pick(table, row, column):
    found = 0
    for r, values in enumerate(table):
        for c, value in enumerate(values):
            found = found + jnp.where((row == r) & (column == c), value, 0)
    return found


def kernel(
    mp,
    T,
    len_ref,
    x_ref,
    dy_ref,
    g1_ref,
    g2_ref,
    cos_ref,
    sin_ref,
    wq_ref,
    wk_ref,
    wv_ref,
    wo_ref,
    wg_ref,
    wu_ref,
    wd_ref,
    out_ref,
    dx_ref,
    ga_ref,
    gm_ref,
    fin_ref,
    w,
    n1,
    n2,
    n2t,
    dyb,
    q,
    k,
    v,
    kt,
    vt,
    ctx,
    heads_t,
    lse,
    mask,
    hb,
    turned_rows,
    made,
    acc,
    res,
    dn,
    dk_sum,
    dv_sum,
    gbuf,
    r1,
    r2,
    r3,
    r4,
    total,
    gain_in,
    staged,
    own_sem,
    z_send,
    z_recv,
    g_send,
    g_recv,
    s_send,
    s_recv,
    h_send,
    h_recv,
    fin_sem,
    f_send,
    f_recv,
    gain_send,
    gain_recv,
    out_sem,
    credit,
):
    seq, width = x_ref.shape[1], x_ref.shape[2]
    half, quarter, eighth = width // 2, width // 4, width // 8
    blocks = [(a, min(a + 256, T)) for a in range(0, T, 256)]
    dp_at, z = lax.axis_index("dp"), lax.axis_index("mp")
    core, bit1, bit2 = dp_at % 2, (dp_at // 2) % 2, (dp_at // 4) % 2
    partner = dp_at + 1 - 2 * core
    flip1, flip2 = dp_at + 2 - 4 * bit1, dp_at + 4 - 8 * bit2
    near = jnp.where(core == 0, flip1, flip2)
    far = jnp.where(core == 0, flip2, flip1)
    near_bit = jnp.where(core == 0, bit1, bit2)
    far_bit = jnp.where(core == 0, bit2, bit1)
    table = order_table(mp)
    units_f, units = 2 * mp, 3 * mp

    def at(start, size):
        return pl.ds(pl.multiple_of(start, 16), size)

    half_at = core * half
    quarter_at = half_at + far_bit * quarter
    eighth_at = quarter_at + near_bit * eighth
    half_rows, quarter_rows, eighth_rows = at(half_at, half), at(quarter_at, quarter), at(eighth_at, eighth)
    colour_rows = at(half_at + (bit1 + bit2) % 2 * quarter, quarter)
    widening = ((near, eighth_rows), (far, quarter_rows), (partner, half_rows))
    brief = ((near, colour_rows), (partner, half_rows))

    def remote(src, dst, send, recv, dp_to, z_to):
        return pltpu.make_async_remote_copy(
            src_ref=src,
            dst_ref=dst,
            send_sem=send,
            recv_sem=recv,
            device_id={"dp": dp_to, "mp": z_to},
            device_id_type=MESH,
        )


    def hops(kind):
        return widening if STEPS[kind] == 3 else brief

    def along(kind, shard, side):
        part = w.at[kind, shard, hops(kind)[0][1]]
        return remote(part, part, z_send.at[kind, shard, side], z_recv.at[kind, shard], dp_at, z + 1 - 2 * side)

    def across(kind, shard, stage):
        to, rows = hops(kind)[stage]
        part = w.at[kind, shard, rows]
        return remote(part, part, g_send.at[kind, shard, stage], g_recv.at[kind, shard, stage], to, z)

    def send_own(kind):
        for side, there in ((0, z + 1 < mp), (1, z > 0)):
            pl.when(there)(lambda side=side: along(kind, z, side).start())

    def pass_on(kind, distance):
        for side, shard, there, onward in (
            (0, z - distance, z - distance >= 0, z + 1 < mp),
            (1, z + distance, z + distance < mp, z > 0),
        ):

            @pl.when(there)
            def _(shard=shard, side=side, onward=onward):
                along(kind, shard, side).wait_recv()
                pl.when(onward)(lambda: along(kind, shard, side).start())

    def gather(kind, j, stage):
        shard = pick(table, z, j)
        if stage > 0:
            across(kind, shard, stage - 1).wait_recv()
        if stage < STEPS[kind]:
            across(kind, shard, stage).start()

    def gather_drain():
        for kind in range(3):

            def each(shard, carry, kind=kind):
                for side, there in ((0, (shard <= z) & (z + 1 < mp)), (1, (shard >= z) & (z > 0))):
                    pl.when(there)(lambda side=side: along(kind, shard, side).wait_send())

                @pl.when(shard != z)
                def _():
                    for stage in range(STEPS[kind]):
                        across(kind, shard, stage).wait_send()

                return carry

            lax.fori_loop(0, mp, each, 0)


    def shard_of(u):
        if isinstance(u, int) and u >= units_f or not isinstance(u, int):
            return (z + 1 + (u - units_f)) % mp
        return pick(table, z, u // 2)

    def kind_of(u):
        return 1 + u % 2 if u < units_f else 0

    narrowing = ((partner, 1 - core, half), (far, 1 - far_bit, quarter), (near, 1 - near_bit, eighth))
    kept = (half_at, far_bit * quarter, near_bit * eighth)
    stores = (gbuf, r1, r2, r3)

    def give(u, stage):
        to, which, size = narrowing[stage]
        return remote(
            stores[stage].at[u % SLOTS[stage], at(which * size, size)],
            stores[stage + 1].at[u % SLOTS[stage + 1]],
            s_send.at[u, stage],
            s_recv.at[u, stage],
            to,
            z,
        )

    def start_give(u, stage):
        late = u >= SLOTS[stage + 1]
        if isinstance(late, bool):
            if late:
                pl.semaphore_wait(credit.at[stage], 1)
        else:
            pl.when(late)(lambda: pl.semaphore_wait(credit.at[stage], 1))
        give(u, stage).start()

    def release(u, stage):
        if u + SLOTS[stage + 1] < units:
            pl.semaphore_signal(
                credit.at[stage], inc=1, device_id={"dp": narrowing[stage][0], "mp": z}, device_id_type=MESH
            )

    def take(u, stage):
        copy = give(u, stage)
        copy.wait_recv()
        copy.wait_send()
        mine, came = stores[stage], stores[stage + 1]
        here, there = u % SLOTS[stage], u % SLOTS[stage + 1]

        def add(i, carry):
            to = at(i * eighth, eighth)
            sums = mine[here, at(kept[stage] + i * eighth, eighth), :].astype(f32) + came[there, to, :].astype(f32)
            came[there, to, :] = sums.astype(bf16)
            return carry

        lax.fori_loop(0, (4, 2, 1)[stage], add, 0)
        if stage > 0:
            release(u, stage - 1)
        if stage < 2:
            start_give(u, stage + 1)
            return
        shard = shard_of(u)

        @pl.when(shard == z)
        def _():
            r4[kind_of(u), z] = r3[there]

        pl.when(shard != z)(lambda: home(u).start())

    def home(u):
        kind = kind_of(u)
        return remote(r3.at[u], r4.at[kind, z], h_send.at[u], h_recv.at[kind, z], dp_at, shard_of(u))

    def home_drain():
        for u in range(units):
            pl.when(shard_of(u) != z)(lambda u=u: home(u).wait_send())


    def fin_own(kind):
        return pltpu.make_async_copy(total.at[kind], fin_ref.at[kind, eighth_rows], fin_sem.at[kind])

    def fin_across(kind, stage):
        to, rows = widening[stage]
        src = total.at[kind] if stage == 0 else fin_ref.at[kind, rows]
        return remote(src, fin_ref.at[kind, rows], f_send.at[kind, stage], f_recv.at[kind, stage], to, z)

    def finish(kind, stage):
        if stage == 0:
            for src in range(mp):

                @pl.when(z != src)
                def _(src=src):
                    remote(r3.at[0], r4.at[kind, src], h_send.at[0], h_recv.at[kind, src], dp_at, src).wait_recv()

            sums = r4[kind, 0].astype(f32)
            for src in range(1, mp):
                sums = sums + r4[kind, src].astype(f32)
            total[kind] = sums.astype(bf16)
            fin_own(kind).start()
        else:
            if stage == 1:
                fin_own(kind).wait()
            fin_across(kind, stage - 1).wait_recv()
        if stage < 3:
            fin_across(kind, stage).start()

    def finish_drain(kind):
        for stage in range(3):
            fin_across(kind, stage).wait_send()


    def gain_copy(stage):
        to = (partner, far, near)[stage]
        return remote(gain_in.at[0], gain_in.at[1 + stage], gain_send.at[stage], gain_recv.at[stage], to, z)

    def gain_along(i):
        return remote(
            gain_in.at[0], gain_in.at[3 + i], gain_send.at[2 + i], gain_recv.at[2 + i], dp_at, (z + i) % mp
        )

    def gain_step(stage):
        if stage in (1, 2, 3):
            gain_copy(stage - 1).wait()
            gain_in[0] = gain_in[0] + gain_in[stage]
        if stage < 3:
            gain_copy(stage).start()
        elif stage == 3:
            for i in range(1, mp):
                gain_along(i).start()
        else:
            for i in range(1, mp):
                gain_along(i).wait()
            sums = gain_in[0]
            for i in range(1, mp):
                sums = sums + gain_in[3 + i]
            ga_ref[...] = sums[0]
            gm_ref[...] = sums[1]

    move = {"s": send_own, "z": pass_on, "g": gather, "t": take, "f": finish, "n": gain_step}

    def place(part, step, i):
        for at_step in range(mp):
            acts = PLAN.get((part, at_step, i))
            if acts is None:
                continue

            def run(acts=acts):
                for name, *what in acts:
                    move[name](*what)

            if isinstance(step, int):
                if step == at_step:
                    run()
            else:
                pl.when(step == at_step)(run)


    barrier = pltpu.get_barrier_semaphore()
    for to in (partner, near, far):
        pl.semaphore_signal(barrier, inc=1, device_id={"dp": to, "mp": z}, device_id_type=MESH)
    for i in range(1, mp):
        pl.semaphore_signal(
            barrier, inc=1, device_id={"dp": dp_at, "mp": (z + i) % mp}, device_id_type=MESH
        )
    cols = wq_ref.shape[0]
    hidden = wg_ref.shape[1]
    first = width - hidden
    rest = hidden - first
    pieces = [(ref, w.at[0, z, pl.ds(i * cols, cols)]) for i, ref in enumerate((wq_ref, wk_ref, wv_ref, wo_ref))]
    pieces += [
        (wg_ref, w.at[1, z, :, pl.ds(0, hidden)]),
        (wu_ref.at[:, pl.ds(0, first)], w.at[1, z, :, pl.ds(hidden, first)]),
        (wd_ref, w.at[2, z, pl.ds(0, hidden)]),
    ]
    stripes = width // rest
    tall = width // stripes
    pieces += [
        (wu_ref.at[pl.ds(j * tall, tall), pl.ds(first, rest)], w.at[2, z, pl.ds(hidden, tall), pl.ds(j * rest, rest)])
        for j in range(stripes)
    ]
    own = [pltpu.make_async_copy(src, dst, own_sem.at[i]) for i, (src, dst) in enumerate(pieces)]
    for copy in own:
        copy.start()

    lane = iota((T, 128), 1)
    lower = lane < 64
    low = (lane % 64) < 32
    length = len_ref[z]
    full = seq // 16 * 16

    def padded(ref):
        tail = jnp.broadcast_to(ref[0, full:seq, :].astype(f32), (T - full, width))
        tail = jnp.where(iota((T - full, width), 0) < seq - full, tail, 0.0).astype(bf16)
        return jnp.concatenate([ref[0, 0:full, :], tail], axis=0)

    def scale_of(rows_in):
        return lax.rsqrt(jnp.mean(rows_in * rows_in, axis=-1, keepdims=True) + EPS)

    def gain(ref):
        return ref[...].reshape(1, width)

    x = padded(x_ref).astype(f32)
    n1[...] = (x * scale_of(x) * gain(g1_ref)).astype(bf16)
    for copy in own:
        copy.wait()
    pl.semaphore_wait(barrier, 3 + mp - 1)
    place("P", 0, 0)

    acc[...] = x
    dyb[...] = jnp.where(iota((T, width), 0) < length, padded(dy_ref).astype(f32), 0.0).astype(bf16)
    key_at, query_at = iota((T, T), 0), iota((T, T), 1)
    mask[...] = jnp.where((key_at <= query_at) & (key_at < length), 0.0, NEG)
    heads_t[...] = jnp.zeros_like(heads_t)


    def attention(step, carry):
        place("A", step, 0)
        cos, sin = cos_ref[...], sin_ref[...]
        s = pick(table, z, step)
        wa = w.at[0, s]
        qkv = nt(n1[...], wa[0:640, :])
        tiles = [qkv[:, 128 * i : 128 * i + 128] for i in range(5)]
        t0, t1, t2 = (t * cos + turned(t, low) * sin for t in tiles[0:3])
        t0, t1s = swap(t0), swap(t1)
        q[s, 0] = jnp.where(lower, 0.0, t0 * 0.125).astype(bf16)
        q[s, 1] = (jnp.where(lower, t0, t1s) * 0.125).astype(bf16)
        k[s, 0] = jnp.where(lower, 0.0, t1).astype(bf16)
        k[s, 1] = t2.astype(bf16)
        t3, t4 = swap(tiles[3]), swap(tiles[4])
        v[s, 0] = jnp.where(lower, 0.0, t3).astype(bf16)
        v[s, 1] = jnp.where(lower, t3, t4).astype(bf16)
        place("A", step, 1)
        for tile in range(2):
            kt[s, tile] = k[s, tile].T
            vt[tile] = v[s, tile].T
        for h, (tile, side) in enumerate(HEADS):
            qh = q[s, tile]
            if tile == 1:
                qh = jnp.where(lower if side == 0 else ~lower, qh, jnp.zeros_like(qh))
            at_row = 128 * tile + 64 * side
            for a, b in blocks:
                scores = nt(k[s, tile, 0:b, :], qh[a:b]) + mask[0:b, a:b]
                peak = jnp.max(scores, axis=0, keepdims=True)
                e = jnp.exp(scores - peak)
                norm = jnp.sum(e, axis=0, keepdims=True)
                c = nn(vt[tile, 64 * side : 64 * side + 64, 0:b], e.astype(bf16))
                heads_t[at_row : at_row + 64, a:b] = c * (1.0 / norm)
                lse[s, h : h + 1, a:b] = peak + jnp.log(norm)
            place("A", step, 2 + h)
        c = heads_t[...].astype(bf16)
        ctx[s] = c
        acc[...] += nn(c.T, wa[512:768, :])
        return carry

    lax.fori_loop(0, mp, attention, 0)

    x1 = acc[...]
    res[...] = x1
    normed = (x1 * scale_of(x1) * gain(g2_ref)).astype(bf16)
    n2[...] = normed
    n2t[...] = normed.T
    dn[...] = jnp.zeros_like(dn)


    def feed(step, carry):
        place("F", step, 0)
        s = pick(table, z, step)
        w1, w2 = w.at[1, s], w.at[2, s]
        u0, u1 = 2 * step, 2 * step + 1
        gu = nn(n2[...], w1[...])
        late = nn(n2[:, 0:256], w2[512:768, 0:256])
        for j in range(1, 3):
            late = late + nn(n2[:, 256 * j : 256 * j + 256], w2[512:768, 256 * j : 256 * j + 256])
        dh = nt(dyb[...], w2[0:512, :])
        for i in range(2):
            part = slice(256 * i, 256 * i + 256)
            gate = gu[:, part]
            up = gu[:, 512:768] if i == 0 else late
            dhid = dh[:, part]
            sigma = 1.0 / (1.0 + jnp.exp(-gate))
            active = gate * sigma
            hb[step, :, part] = (active * up).astype(bf16)
            made[:, part] = (dhid * up * sigma * (1.0 + gate * (1.0 - sigma))).astype(bf16)
            made[:, 512 + 256 * i : 768 + 256 * i] = (dhid * active).astype(bf16)
        place("F", step, 1)
        gbuf[u0 % SLOTS[0]] = nn(n2t[...], made[:, 0:768]).astype(bf16)
        start_give(u0, 0)
        place("F", step, 2)
        turned_rows[0:512, :] = hb[step].T
        dn[...] += nt(made[:, 0:768], w1[...])
        place("F", step, 3)
        gbuf[u1 % SLOTS[0], 0:512, :] = nn(turned_rows[0:512, :], dyb[...]).astype(bf16)
        for j in range(3):
            part = slice(256 * j, 256 * j + 256)
            gbuf[u1 % SLOTS[0], 512:768, part] = nn(n2t[part, :], made[:, 768:1024]).astype(bf16)
        start_give(u1, 0)
        place("F", step, 4)
        for j in range(3):
            part = slice(256 * j, 256 * j + 256)
            dn[:, part] += nt(made[:, 768:1024], w2[512:768, part])
        return carry

    lax.fori_loop(0, mp, feed, 0)

    place("M", 0, 0)
    x1 = res[...]
    scale = scale_of(x1)
    hat = x1 * scale
    d2 = dn[...]
    gain_in[0] = jnp.zeros_like(gain_in[0])
    gain_in[0, 1:2, :] = jnp.sum(d2 * hat, axis=0, keepdims=True)
    e = d2 * gain(g2_ref)
    dx1 = dyb[...].astype(f32) + scale * (e - hat * jnp.mean(e * hat, axis=-1, keepdims=True))
    res[...] = dx1
    n2[...] = dx1.astype(bf16)
    dn[...] = jnp.zeros_like(dn)
    heads_t[192:256, :] = jnp.zeros((64, T), f32)


    def back(step, carry):
        u = units_f + step
        slot = u % SLOTS[0]
        place("B", step, 0)
        cos, sin = cos_ref[...], sin_ref[...]
        s = shard_of(u)
        wa = w.at[0, s]
        dc = nt(n2[...], wa[512:768, :])
        dc = [jnp.where(lower, 0.0, dc[:, 0:128]).astype(bf16), dc[:, 128:256].astype(bf16)]
        for tile in range(2):
            dk_sum[tile] = jnp.zeros((T, 128), f32)
            dv_sum[tile] = jnp.zeros((T, 128), f32)
        for h, (tile, side) in enumerate(HEADS):
            qh, dch = q[s, tile], dc[tile]
            if tile == 1:
                here = lower if side == 0 else ~lower
                qh = jnp.where(here, qh, jnp.zeros_like(qh))
                dch = jnp.where(here, dch, jnp.zeros_like(dch))
            for i, (a, b) in enumerate(blocks):
                scores = nt(k[s, tile, 0:b, :], qh[a:b]) + mask[0:b, a:b]
                p = jnp.exp(scores - lse[s, h : h + 1, a:b])
                dprob = nt(v[s, tile, 0:b, :], dch[a:b])
                delta = jnp.sum(p * dprob, axis=0, keepdims=True)
                ds = (p * (dprob - delta)).astype(bf16)
                dv_sum[tile, 0:b, :] += nn(p.astype(bf16), dch[a:b])
                dk_sum[tile, 0:b, :] += nn(ds, qh[a:b])
                heads_t[64 * h : 64 * h + 64, a:b] = nn(kt[s, tile, 64 * side : 64 * side + 64, 0:b], ds)
                if i == 1:
                    place("B", step, 1 + 2 * h)
            place("B", step, 2 + 2 * h)

        def unturned(t):
            return t * cos - turned(t, low) * sin

        dq01 = unturned(heads_t[0:128, :].T * 0.125)
        dq2 = unturned(heads_t[128:256, :].T * 0.125)
        made[:, 0:128] = dq01.astype(bf16)
        made[:, 128:256] = jnp.where(lower, dq2, unturned(dk_sum[0])).astype(bf16)
        made[:, 256:384] = unturned(dk_sum[1]).astype(bf16)
        dv0, dv1 = swap(dv_sum[0]), swap(dv_sum[1])
        made[:, 384:512] = jnp.where(lower, dv0, dv1).astype(bf16)
        made[:, 512:640] = jnp.where(lower, dv1, 0.0).astype(bf16)
        turned_rows[...] = made[:, 0:640].T
        place("B", step, 7)
        gbuf[slot, 0:576, :] = nn(turned_rows[0:576, :], n1[...]).astype(bf16)
        gbuf[slot, 576:768, :] = nn(ctx[s, 64:256, :], n2[...]).astype(bf16)
        start_give(u, 0)
        place("B", step, 8)
        dn[...] += nn(made[:, 0:640], wa[0:640, :])
        return carry

    lax.fori_loop(0, mp, back, 0)


    place("E", 0, 0)
    x = padded(x_ref).astype(f32)
    scale = scale_of(x)
    hat = x * scale
    d1 = dn[...]
    gain_in[0, 0:1, :] = jnp.sum(d1 * hat, axis=0, keepdims=True)
    place("E", 0, 1)
    e = d1 * gain(g1_ref)
    dx = res[...] + scale * (e - hat * jnp.mean(e * hat, axis=-1, keepdims=True))
    staged[:, 0, :] = dx[0:seq]
    out_dx = pltpu.make_async_copy(staged, dx_ref, out_sem.at[0])
    out_dx.start()
    place("E", 0, 2)
    for j in range(mp):
        acc[...] += nn(hb[j], w[2, pick(table, z, j), 0:512, :])
        place("E", 0, 3 + j)
    out_dx.wait()
    staged[:, 0, :] = acc[0:seq, :]
    out_y = pltpu.make_async_copy(staged, out_ref, out_sem.at[1])
    out_y.start()
    place("E", 0, 3 + mp)
    gather_drain()
    home_drain()
    for kind in range(3):
        finish_drain(kind)
    out_y.wait()


def rotary(rows):
    position = np.arange(rows).astype(np.float32)
    index = np.arange(HEAD // 2).astype(np.float32)
    freq = (np.float32(10000.0) ** (np.float32(-2.0) * index / np.float32(HEAD))).astype(np.float32)
    angle = position[:, None] * freq[None, :]
    angle = np.concatenate([angle] * 4, axis=-1)
    return np.cos(angle).astype(np.float32), np.sin(angle).astype(np.float32)


def layer(mp, lengths, tokens, cotangent, gain1, gain2, weights):
    _, seq, width = tokens.shape
    T = (seq + 15) // 16 * 16
    cosine, sine = rotary(T)
    vmem, anywhere = pl.BlockSpec(memory_space=pltpu.VMEM), pl.BlockSpec(memory_space=pl.ANY)
    V, DMA = pltpu.VMEM, pltpu.SemaphoreType.DMA
    half, quarter, eighth = width // 2, width // 4, width // 8
    scratch = [
        V((3, mp, width, width), bf16),
        V((T, width), bf16),
        V((T, width), bf16),
        V((width, T), bf16),
        V((T, width), bf16),
        V((mp, 2, T, 128), bf16),
        V((mp, 2, T, 128), bf16),
        V((mp, 2, T, 128), bf16),
        V((mp, 2, 128, T), bf16),
        V((2, 128, T), bf16),
        V((mp, 256, T), bf16),
        V((256, T), f32),
        V((mp, 8, T), f32),
        V((T, T), f32),
        V((mp, T, 512), bf16),
        V((640, T), bf16),
        V((T, 1024), bf16),
        V((T, width), f32),
        V((T, width), f32),
        V((T, width), f32),
        V((2, T, 128), f32),
        V((2, T, 128), f32),
        V((SLOTS[0], width, width), bf16),
        V((SLOTS[1], half, width), bf16),
        V((SLOTS[2], quarter, width), bf16),
        V((SLOTS[3], eighth, width), bf16),
        V((3, mp, eighth, width), bf16),
        V((3, eighth, width), bf16),
        V((3 + mp, 8, width), f32),
        V((seq, 1, width), f32),
        DMA((10,)),
        DMA((3, mp, 2)),
        DMA((3, mp)),
        DMA((3, mp, 3)),
        DMA((3, mp, 3)),
        DMA((3 * mp, 3)),
        DMA((3 * mp, 3)),
        DMA((3 * mp,)),
        DMA((3, mp)),
        DMA((3,)),
        DMA((3, 3)),
        DMA((3, 3)),
        DMA((2 + mp,)),
        DMA((2 + mp,)),
        DMA((2,)),
        pltpu.SemaphoreType.REGULAR((3,)),
    ]
    return pl.pallas_call(
        functools.partial(kernel, mp, T),
        out_shape=(
            jax.ShapeDtypeStruct((seq, 1, width), f32),
            jax.ShapeDtypeStruct((seq, 1, width), f32),
            jax.ShapeDtypeStruct((width,), f32),
            jax.ShapeDtypeStruct((width,), f32),
            jax.ShapeDtypeStruct((3, width, width), bf16),
        ),
        in_specs=[pl.BlockSpec(memory_space=pltpu.SMEM)] + [vmem] * 6 + [anywhere] * 7,
        out_specs=[anywhere, anywhere, vmem, vmem, anywhere],
        scratch_shapes=scratch,
        compiler_params=pltpu.CompilerParams(
            collective_id=0, has_side_effects=True, vmem_limit_bytes=63 * 2**20
        ),
    )(lengths, tokens, cotangent, gain1, gain2, jnp.asarray(cosine), jnp.asarray(sine), *weights)


def per_device(mp, dp, tokens, lengths, gain1, gain2, wq, wk, wv, wo, wg, wu, wd, cotangent):
    _, seq, width = tokens.shape
    weights = (wq.T, wk.T, wv.T, wo, wg, wu, wd)
    out, dx, gain_a, gain_m, fin = layer(mp, lengths, tokens, cotangent, gain1, gain2, weights)
    if dp > 8:
        groups = [[8 * i + j for i in range(dp // 8)] for j in range(8)]
        fin, gain_a, gain_m = lax.psum((fin.astype(f32), gain_a, gain_m), "dp", axis_index_groups=groups)
    fin = fin.astype(f32)
    cols, hidden = wq.shape[1], wg.shape[1]
    first = width - hidden
    rest = hidden - first
    late = fin[2, hidden:]
    late = jnp.concatenate([late[:, rest * j : rest * j + rest] for j in range(width // rest)], axis=0)
    return (
        out.reshape(1, seq, width),
        dx.reshape(1, seq, width),
        gain_a,
        gain_m,
        fin[0, 0:cols].T,
        fin[0, cols : 2 * cols].T,
        fin[0, 2 * cols : 3 * cols].T,
        fin[0, 3 * cols :],
        fin[1, :, 0:hidden],
        jnp.concatenate([fin[1, :, hidden:], late], axis=1),
        fin[2, 0:hidden],
    )


def solution(mesh):
    rows, cols, items = P("mp", None), P(None, "mp"), P(("dp", "mp"), None, None)
    return jax.shard_map(
        functools.partial(per_device, mesh.shape["mp"], mesh.shape["dp"]),
        mesh=mesh,
        in_specs=(items, P("dp"), P(), P(), cols, cols, cols, rows, cols, cols, rows, items),
        out_specs=(items, items, P(), P(), cols, cols, cols, rows, cols, cols, rows),
        check_vma=False,
    )
```

time: 252 us -> 179 us (0.71)
  Pallas kernels: 208 us -> 164 us
  local copies, waits for them, and re-layouts: 36.4 us -> 9.5 us
    pallas_call x1, Pallas kernels: 208 us -> 164 us  [layer(): pl.pallas_call(functools.partial(kernel, mp, T), out_shape=(jax.ShapeDtyp...]
    unnamed x27 -> x12, local copies, waits for them, and re-layouts: 17.1 us -> 5.32 us
    slice x12 -> x1, local copies, waits for them, and re-layouts: 11.3 us -> 0.06 us  [per_device(): late[:, rest * j:rest * j + rest]]
    broadcast_in_dim x4 -> x0, local copies, waits for them, and re-layouts: 4.31 us -> none  [the longest x1 1.6 us: per_device(): out[None, :seq]]
where the time goes in v2:
time: 179 us; the launch traced here: 178 us
  Pallas kernels  164 us (92%)
  local copies, waits for them, and re-layouts  9.5 us (5%)
  other arithmetic  3.98 us (2%)
    pallas_call x1, Pallas kernels, layer(): pl.pallas_call(functools.partial(kernel, mp, T), out_shape=(jax.ShapeDtyp...  164 us
    unnamed x12, local copies, waits for them, and re-layouts  5.32 us

profile of v2, /device:TPU:0, one launch (start us, length us, event | category | flops | bytes accessed | tf_op | source)
XLA Modules:
  0.0 178.3 jit_solution(9412656691636433661)
XLA Ops:
  0.6 164.2 %shard_map.221 = (f32[577,1,768]{2,1,0:T(1,128)}, f32[577,1,768]{2,1,0:T(1,128)}, f32[768]{0:T(1024)}, f32[768]{0:T(1024)}, bf16[3,768,768]{2,1,0:T(8,128)(2,1)}) custom-call(s32[4]{0:T(128)} %len_ref.1, bf16[1,577,768]{2,1,0:T(8,128)(2,1)} %x_ref.1, bf16[1,577,768]{2,1,0:T(8,128)(2,1)} %dy_ref.1, f32[768]{0:T(1024)} %g1_ref.1, f32[768]{0:T(1024)} %g2_ref.1, ...), custom_call_target="tpu_custom_call" | custom-call | tf_op jit(solution)/shard_map/pallas_call | solution.py:724
  164.8 2.6 %convert_element_type.3 = f32[3,768,768]{2,1,0:T(8,128)S(1)} convert(bf16[3,768,768]{2,1,0:T(8,128)(2,1)} %get-tuple-element.20) | non-fusion elementwise | flops 1769472 | bytes 10616832 | tf_op jit(solution)/shard_map/convert_element_type | solution.py:749
  167.4 1.4 slice_bitcast_fusion.4
  168.9 1.3 slice_bitcast_fusion.1
  170.2 0.1 slice_bitcast_fusion.2
  170.3 0.1 fusion
  170.3 0.1 slice_bitcast_fusion.3
  170.4 1.4 maximum_maximum_fusion
  171.8 0.0 copy-start.1
  171.8 1.2 slice_bitcast_fusion
  173.0 0.8 copy-done.1
  173.8 0.0 copy-start
  173.8 1.2 copy.29
  175.0 0.9 copy-done
  175.9 0.0 copy-start.3
  175.9 0.0 copy-start.2
  175.9 1.2 copy.30
  177.1 0.0 copy-done.3
  177.1 0.6 copy.31
  177.7 0.0 copy-done.2
  177.7 0.6 copy.32
Async XLA Ops:
  171.8 2.0 %copy-start.1 = (f32[577,1,768]{2,1,0:T(1,128)S(1)}, f32[577,1,768]{2,1,0:T(1,128)}, u32[]{:S(2)}) copy-start(f32[577,1,768]{2,1,0:T(1,128)} %get-tuple-element.16) | copy-start | bytes 5317636
  173.8 2.1 %copy-start = (f32[577,1,768]{2,1,0:T(1,128)S(1)}, f32[577,1,768]{2,1,0:T(1,128)}, u32[]{:S(2)}) copy-start(f32[577,1,768]{2,1,0:T(1,128)} %get-tuple-element.17) | copy-start | bytes 5317636
  175.9 1.2 copy-start.3
  175.9 1.8 %copy-start.2 = (f32[768]{0:T(1024)S(1)}, f32[768]{0:T(1024)}, u32[]{:S(2)}) copy-start(f32[768]{0:T(1024)} %get-tuple-element.42) | copy-start | bytes 9220
